TPU v7x, 32 devices: a whole 2x2x4 slice. The times are simulated.
32 devices in a mesh: ctx: 8 (over y, x, core), head: 4 (over z).
Axes of the slice: x: 2, y: 2, z: 4, core: 2. Of those that a mesh axis runs over, the one named last changes fastest.
Arguments:
- ssm_input: bfloat16 [2048, 8192], P('ctx', 'head'), may hold values from -6 to 6
- gate_input: bfloat16 [2048, 8192], P('ctx', 'head'), may hold values from -6 to 6
- step_raw: float32 [2048, 128], P('ctx', 'head'), may hold values from -4 to 4
- b_matrix: bfloat16 [2048, 1024], P('ctx', 'head'), may hold values from -6 to 6
- c_matrix: bfloat16 [2048, 1024], P('ctx', 'head'), may hold values from -6 to 6
- step_bias: float32 [128], P('head'), may hold values from -6 to -4
- log_rate: float32 [128], P('head')
- skip_gain: float32 [128], P('head'), may hold values from 0.5 to 1.5
- norm_weight: float32 [8192], P('head'), may hold values from 0.5 to 1.5
- doc_resets: int32 [2048], P('ctx'), may hold values from 0 to 1, as said below
- grad_output: bfloat16 [2048, 8192], P('ctx', 'head'), may hold values from -6 to 6
Outputs:
- grad_input: bfloat16 [2048, 8192], P('ctx', 'head')
- grad_gate: bfloat16 [2048, 8192], P('ctx', 'head')
- grad_step: float32 [2048, 128], P('ctx', 'head')
- grad_b_matrix: float32 [2048, 1024], P('ctx', 'head')
- grad_c_matrix: float32 [2048, 1024], P('ctx', 'head')
Inputs may be any that keep to these rules, and one draw needn't show every extreme that they name: `doc_resets`: exactly 4 positions hold 1, all of them among positions 1 to 127; all others hold 0.
All inputs are finite; a program needn't handle non-finite values.
Results may differ from a plain program's by a relative error of at most 0.001.
Values sent between devices are 32-bit elements; how exact they have to be, the bound alone decides.
A program may use at most 64 MiB of HBM per device.

v0:
```python
import jax
import jax.numpy as jnp
from jax import lax
from jax.sharding import PartitionSpec as P

HEAD_DIM = 64
STATE = 128
SPAN = 256


HIGHEST_PRECISION = lax.Precision.HIGHEST
EPSILON = 1e-05


def carried_in(array, axis, combine, identity):
    size, index = (lax.axis_size(axis), lax.axis_index(axis))
    everything = jax.tree.map(lambda part: lax.all_gather(part, axis), array)
    start = jax.tree.map(
        lambda part, zero: jnp.broadcast_to(jnp.asarray(zero, part.dtype), part.shape),
        array,
        identity,
    )

    def turn(k, before):
        at = size - 1 - k
        reached = at > index
        new = combine(before, jax.tree.map(lambda part: part[at], everything))
        return jax.tree.map(lambda a, b: jnp.where(reached, a, b), new, before)

    return lax.fori_loop(0, size, turn, start)


def span_mix(x_span, dt_span, b_span, c_span, log_cum, segment):
    log_rows = jnp.moveaxis(log_cum, 0, -1)
    spread = log_rows[..., :, None] - log_rows[..., None, :]
    places = jnp.arange(x_span.shape[0], dtype=jnp.int32)
    keep_mask = (
        (places[:, None] >= places[None, :]) & (segment[:, None] == segment[None, :])
    ).astype(jnp.float32)
    masked = jnp.exp(jnp.minimum(spread, 0.0)) * keep_mask
    scores = jnp.einsum("tgn,sgn->gts", c_span, b_span, precision=HIGHEST_PRECISION)
    weights = scores[:, None] * masked * jnp.moveaxis(dt_span, 0, -1)[..., None, :]
    return jnp.einsum("ghts,sghp->tghp", weights, x_span, precision=HIGHEST_PRECISION)


def block_decays(dt_spans, segment, decay_rate):
    log_cum = jnp.cumsum(dt_spans * decay_rate, axis=1)
    closing = segment[:, -1]
    through = jnp.exp(log_cum[:, -1]) * (closing == 0).astype(jnp.float32)[:, None, None]
    return (log_cum, closing, through)


def local_states(x_spans, dt_spans, b_spans, segment, decay_rate):
    log_cum, closing, through = block_decays(dt_spans, segment, decay_rate)
    same_doc = (segment == closing[:, None]).astype(jnp.float32)
    tail_decay = jnp.exp(log_cum[:, -1:] - log_cum) * same_doc[:, :, None, None]
    added_terms = jnp.einsum(
        "kqgh,kqghp,kqgn->kghpn",
        tail_decay * dt_spans,
        x_spans,
        b_spans,
        precision=HIGHEST_PRECISION,
    )

    def advance(carried_pair, item_pair):
        carry_state, product = carried_pair
        decay_now, fresh_state = item_pair
        return (
            (decay_now[..., None, None] * carry_state + fresh_state, product * decay_now),
            carry_state,
        )

    initial = (
        jnp.zeros(added_terms.shape[1:], jnp.float32),
        jnp.ones(through.shape[1:], jnp.float32),
    )
    (final_state, product), starts = lax.scan(advance, initial, (through, added_terms))
    return (starts, final_state, product)


def output_part(x_spans, dt_spans, b_spans, c_spans, segment, decay_rate, starts, entry_state):
    log_cum, closing, through = block_decays(dt_spans, segment, decay_rate)

    def rolling(product, decay_now):
        return (product * decay_now, product)

    _, before = lax.scan(rolling, jnp.ones(through.shape[1:], jnp.float32), through)
    full_start = starts + before[..., None, None] * entry_state[None]
    opened = (segment == 0).astype(jnp.float32)
    entry_decay = jnp.exp(log_cum) * opened[:, :, None, None]
    carried = (
        jnp.einsum("kqgn,kghpn->kqghp", c_spans, full_start, precision=HIGHEST_PRECISION)
        * entry_decay[..., None]
    )
    mix_block = jax.checkpoint(lambda pieces: span_mix(*pieces))
    inner_part = lax.map(mix_block, (x_spans, dt_spans, b_spans, c_spans, log_cum, segment))
    return inner_part + carried


def compose(earlier, later):
    decay_early, sum_early = earlier
    decay_late, sum_late = later
    return (decay_early * decay_late, decay_late[..., None, None] * sum_early + sum_late)


def body(
    ssm_input,
    gate_input,
    step_raw,
    b_matrix,
    c_matrix,
    step_bias,
    log_rate,
    skip_gain,
    norm_weight,
    doc_resets,
    grad_output,
):
    tokens_here = ssm_input.shape[0]
    heads_here = step_raw.shape[1]
    groups_here = b_matrix.shape[1] // STATE
    per_group = heads_here // groups_here
    spans = tokens_here // SPAN
    x_float = ssm_input.astype(jnp.float32)
    gate_float = gate_input.astype(jnp.float32)
    shifted = step_raw + step_bias[None, :]
    step_size = jax.nn.softplus(shifted)
    decay_rate = (-jnp.exp(log_rate)).reshape(groups_here, per_group)
    x_spans = x_float.reshape(spans, SPAN, groups_here, per_group, HEAD_DIM)
    dt_spans = step_size.reshape(spans, SPAN, groups_here, per_group)
    b_spans = b_matrix.astype(jnp.float32).reshape(spans, SPAN, groups_here, STATE)
    c_spans = c_matrix.astype(jnp.float32).reshape(spans, SPAN, groups_here, STATE)
    segment = jnp.cumsum(doc_resets.reshape(spans, SPAN), axis=1, dtype=jnp.int32)

    def states_call(x_value, dt_value, b_value):
        return local_states(x_value, dt_value, b_value, segment, decay_rate)

    (starts, end_local, through_all), states_back = jax.vjp(states_call, x_spans, dt_spans, b_spans)
    identity = (jnp.ones_like(through_all), jnp.zeros_like(end_local))
    decay_table = lax.all_gather(through_all.reshape(1, heads_here), "ctx", axis=0, tiled=True)
    own_index = lax.axis_index("ctx")
    ctx_count = lax.axis_size("ctx")
    flat_end = end_local.reshape(heads_here, HEAD_DIM, STATE)
    row_ids = jnp.arange(lax.axis_size("ctx") * heads_here, dtype=jnp.int32)
    receiver = row_ids // heads_here
    head_ids = row_ids % heads_here
    devices = jnp.arange(ctx_count, dtype=jnp.int32)
    between = (devices[None, :] > own_index) & (devices[None, :] < receiver[:, None])
    factors = jnp.where(between, decay_table[:, head_ids].T, 1.0)
    weight = jnp.prod(factors, axis=1) * (own_index < receiver).astype(jnp.float32)
    entry_state = lax.psum_scatter(
        weight[:, None, None] * jnp.take(flat_end, head_ids, axis=0),
        "ctx",
        scatter_dimension=0,
        tiled=True,
    ).reshape(end_local.shape)

    def output_call(x_value, dt_value, b_value, c_value, start_value, entry_value):
        return output_part(
            x_value, dt_value, b_value, c_value, segment, decay_rate, start_value, entry_value
        )

    core_part, output_back = jax.vjp(
        output_call, x_spans, dt_spans, b_spans, c_spans, starts, entry_state
    )
    skip_cols = jnp.repeat(skip_gain, HEAD_DIM)[None, :]
    core_out = core_part.reshape(tokens_here, heads_here * HEAD_DIM) + x_float * skip_cols
    gate_sig = jax.nn.sigmoid(gate_float)
    gate_act = gate_float * gate_sig
    gated = core_out * gate_act
    weighted_grad = norm_weight[None, :] * grad_output.astype(jnp.float32)
    norm_width = lax.axis_size("head") * gated.shape[1]
    squares, product = lax.psum(
        (jnp.sum(gated * gated, axis=1), jnp.sum(weighted_grad * gated, axis=1)), "head"
    )
    inv_rms = lax.rsqrt(squares / norm_width + EPSILON)
    grad_gated = (
        inv_rms[:, None] * weighted_grad - gated * (inv_rms**3 * product / norm_width)[:, None]
    )
    grad_core = grad_gated * gate_act
    grad_gate = grad_gated * core_out * gate_sig * (1.0 + gate_float * (1.0 - gate_sig))
    first_grads = output_back(grad_core.reshape(core_part.shape))
    _, exit_adjoint = carried_in((through_all, first_grads[5]), "ctx", compose, identity)
    through_grad = jnp.sum(exit_adjoint * entry_state, axis=(2, 3))
    second_grads = states_back((first_grads[4], exit_adjoint, through_grad))
    grad_input = (first_grads[0] + second_grads[0]).reshape(
        tokens_here, heads_here * HEAD_DIM
    ) + grad_core * skip_cols
    grad_step = (first_grads[1] + second_grads[1]).reshape(
        tokens_here, heads_here
    ) * jax.nn.sigmoid(shifted)
    grad_b_matrix = (first_grads[2] + second_grads[2]).reshape(tokens_here, groups_here * STATE)
    grad_c_matrix = first_grads[3].reshape(tokens_here, groups_here * STATE)
    return (
        grad_input.astype(jnp.bfloat16),
        grad_gate.astype(jnp.bfloat16),
        grad_step,
        grad_b_matrix,
        grad_c_matrix,
    )


def solution(mesh):
    return jax.shard_map(
        body,
        mesh=mesh,
        in_specs=(
            P("ctx", "head"),
            P("ctx", "head"),
            P("ctx", "head"),
            P("ctx", "head"),
            P("ctx", "head"),
            P("head"),
            P("head"),
            P("head"),
            P("head"),
            P("ctx"),
            P("ctx", "head"),
        ),
        out_specs=(
            P("ctx", "head"),
            P("ctx", "head"),
            P("ctx", "head"),
            P("ctx", "head"),
            P("ctx", "head"),
        ),
        check_vma=False,
    )
```

profile of v0, /device:TPU:0, one launch (start us, length us, event | category | flops | bytes accessed | tf_op | source)
XLA Modules:
  0.0 247.7 jit_solution(12051347147732226692)
XLA Ops:
  16.1 10.2 %all-gather.2 = f32[8,1,32]{2,1,0:T(1,128)S(1)} all-gather(f32[1,1,32]{2,1,0:T(1,128)S(1)} %reshape.691), channel_id=1, replica_groups=mesh['ctx'=8,'head'=4] {'ctx'}, dimensions={0}, use_global_device_ids=true | all-gather | bytes 1152 | tf_op jit(solution)/shard_map/all_gather | solution.py:140
  31.2 4.4 %gather_fusion.1 = f32[256,64,128]{2,1,0:T(8,128)} fusion(f32[32,64,128]{2,1,0:T(8,128)S(1)} %bitcast_add_fusion.4, s32[1024]{0:T(1024)S(1)} %pad_clamp_fusion), kind=kCustom, calls=%fused_computation.1 | custom fusion | bytes 16778240 | tf_op jit(solution)/shard_map/jit(_take)/gather | solution.py:152
  35.5 6.2 %select_multiply_fusion = f32[256,64,128]{2,1,0:T(8,128)} fusion(f32[256,64,128]{2,1,0:T(8,128)} %gather_fusion.1, f32[256]{0:T(256)S(1)} %compare_select_fusion.3, pred[256]{0:T(512)(128)(4,1)S(1)} %compare_and_fusion), kind=kLoop, calls=%fused_computation.19 | loop fusion | flops 4194304 | bytes 16778496 | tf_op jit(solution)/shard_map/mul | solution.py:152
  46.8 2.1 fusion.104
  48.8 64.7 %reduce-scatter.2.cloned.1.call-done = f32[32,64,128]{2,1,0:T(8,128)} async-done(((f32[256,64,128]{2,1,0:T(8,128)}), f32[32,64,128]{2,1,0:T(8,128)}) %reduce-scatter.2.cloned.1.call-update) | async-done | bytes 1048592 | tf_op jit(solution)/shard_map/reduce_scatter | solution.py:151
  113.5 2.3 fusion.81
  115.9 6.3 %bitcast_add_fusion.1 = f32[1,256,2,16,64]{1,4,3,2,0:T(8,128)S(1)} fusion(f32[2,16,64,256]{3,2,1,0:T(8,128)S(1)} %fusion.81, bf16[256,2,16,64]{0,3,2,1:T(8,128)(2,1)S(1)} %bitcast.243, f32[2,16,256]{2,1,0:T(8,128)S(1)} %bitcast.264, f32[256,256]{1,0:T(8,128)S(1)} %copy-done.30, f32[2,16,256]{2,1,0:T(8,128)S(1)} %bitcast.258, ...), kind=kOutput, calls=%fused_computation.53 | convolution fusion | flops 1622147072 | bytes 6127616 | tf_op jit(solution)/shard_map/jvp()/while/body/eval_jaxpr/ghts,sghp->tghp/dot_general | solution.py:43
  122.2 2.4 multiply_reduce_fusion.1
  124.6 11.7 %all-reduce.3 = (f32[256]{0:T(256)S(1)}, f32[256]{0:T(256)S(1)}) all-reduce(f32[256]{0:T(256)S(1)} %get-tuple-element.355, f32[256]{0:T(256)S(1)} %get-tuple-element.354), channel_id=1, replica_groups=mesh['ctx'=8,'head'=4] {'head'}, use_global_device_ids=true, to_apply=%region_9.10 | all-reduce | flops 512 | bytes 4096 | tf_op jit(solution)/shard_map/psum | solution.py:173
  136.3 4.4 %fusion.40 = (bf16[256,2048]{0,1:T(8,128)(2,1)}, f32[256,2048]{0,1:T(8,128)S(1)}) fusion(bf16[256,2048]{0,1:T(8,128)(2,1)} %copy-done.3, f32[256,2048]{0,1:T(8,128)} %get-tuple-element.374, bf16[256,2048]{0,1:T(8,128)(2,1)} %copy-done.4, f32[256]{0:T(256)S(1)} %get-tuple-element.389, f32[2048]{0:T(1024)S(1)} %copy-done.38, f32[256]{0:T(256)S(1)} %get-tuple-element.388, ...), kind=kLoop, calls=%fused_computation.52 | loop fusion | flops 11010048 | bytes 10504192 | tf_op jit(solution)/shard_map/convert_element_type | solution.py:196
  140.7 2.1 fusion.43
  143.6 2.8 %convert.7 = f32[256,2,16,64]{0,3,2,1:T(8,128)} convert(bf16[256,2,16,64]{0,3,2,1:T(8,128)(2,1)} %bitcast.244) | non-fusion elementwise | flops 524288 | bytes 3145728 | tf_op jit(solution)/shard_map/transpose(jvp())/while/body/jit(dynamic_index_in_dim)/squeeze | solution.py:96
  147.7 9.9 %all-gather = f32[8,1,2,16]{3,2,1,0:T(2,128)} all-gather(f32[1,1,2,16]{3,2,1,0:T(2,128)} %copy.143), channel_id=2, replica_groups=mesh['ctx'=8,'head'=4] {'ctx'}, dimensions={0}, use_global_device_ids=true | all-gather | bytes 1152 | tf_op jit(solution)/shard_map/all_gather | solution.py:17
  157.7 2.3 copy.161
  161.8 16.2 %fusion.73 = (f32[2,16,256]{2,1,0:T(8,128)}, f32[2,16,256]{2,1,0:T(8,128)}, f32[2,16,256]{2,1,0:T(8,128)}, f32[2,256,256]{2,1,0:T(8,128)S(1)}) fusion(f32[2,16,256]{2,1,0:T(8,128)} %bitcast.257, f32[256,256]{1,0:T(8,128)S(1)} %fusion.78, f32[2,16,256]{2,1,0:T(8,128)} %bitcast.263, f32[2,256,256]{2,1,0:T(8,128)S(1)} %fusion.105, ...), kind=kOutput, calls=%fused_computation.90 | convolution fusion | flops 1650302976 | bytes 5668864 | tf_op jit(solution)/shard_map/transpose(jvp())/while/body/eval_jaxpr/checkpoint/ghts,sghp->tghp/dot_general | solution.py:43
  178.7 2.8 %fusion.62 = f32[1,256,2,128]{1,3,2,0:T(8,128)} fusion(f32[1,256,2,128]{1,3,2,0:T(8,128)S(1)} %convolution_bitcast_fusion, f32[2,16,64,128]{3,2,1,0:T(8,128)S(1)} %bitcast.248, f32[1,256,2,16,64]{1,4,3,2,0:T(8,128)S(1)} %bitcast.239, f32[256,2,16]{0,2,1:T(8,128)S(1)} %copy-done.24), kind=kOutput, calls=%fused_computation.78 | convolution fusion | flops 805896192 | bytes 3702784 | tf_op jit(solution)/shard_map/transpose(jvp(kqgn,kghpn->kqghp))/dot_general | solution.py:92
  183.2 2.2 convolution_bitcast_fusion.1
  185.4 2.6 %fusion.46 = f32[256,2,16]{0,2,1:T(8,128)} fusion(f32[1,256,2,16,64]{1,4,3,2,0:T(8,128)S(1)} %bitcast.240, f32[2,16,64,256]{3,2,1,0:T(8,128)} %copy-done.5), kind=kLoop, calls=%fused_computation.62 | loop fusion | flops 1040384 | bytes 4227072 | tf_op jit(solution)/shard_map/transpose(jvp())/reduce_sum | solution.py:92
  188.1 6.5 %all-gather.5.cloned.1.call-done = f32[16,16,64,128]{3,2,1,0:T(8,128)} async-done(((f32[2,16,64,128]{3,2,1,0:T(8,128)}), f32[16,16,64,128]{3,2,1,0:T(8,128)}) %all-gather.5.cloned.1.call-update) | async-done | bytes 8388624 | tf_op jit(solution)/shard_map/all_gather | solution.py:17
  194.6 17.3 %while.11 = (s32[]{:T(128)}, f32[2,16,64,128]{3,2,1,0:T(8,128)S(1)}, s32[]{:T(128)}, f32[8,2,16]{2,1,0:T(2,128)}, f32[8,2,16,64,128]{4,3,2,1,0:T(8,128)}, /*index=5*/s32[]{:T(128)}, s32[]{:T(128)}, s32[]{:T(128)}, s32[]{:T(128)}) while((s32[]{:T(128)}, f32[2,16,64,128]{3,2,1,0:T(8,128)S(1)}, s32[]{:T(128)}, ...), condition=%wide.region_11.12_spmd.clone, body=%wide.region_10.11_spmd.clone.sunk | while | flops 1048584 | bytes 3146287 | solution.py:30
  211.9 2.2 multiply_reduce_fusion.2
  218.0 7.4 %fusion.45 = f32[256,2,16,64]{0,3,2,1:T(8,128)S(1)} fusion(f32[2,16,64,256]{3,2,1,0:T(8,128)S(1)} %get-tuple-element.391, f32[2,16,256]{2,1,0:T(8,128)S(1)} %bitcast.265, f32[256,256]{1,0:T(8,128)S(1)} %copy-done.29, f32[2,16,256]{2,1,0:T(8,128)S(1)} %bitcast.259, f32[2,256,256]{2,1,0:T(8,128)S(1)} %copy-done.22, f32[256,2,16,64]{0,3,2,1:T(8,128)S(1)} %bitcast.241, ...), kind=kOutput, calls=%fused_computation.59 | convolution fusion | flops 1622147072 | bytes 7176192 | tf_op jit(solution)/shard_map/transpose(jvp())/while/body/eval_jaxpr/checkpoint/ghts,sghp->tghp/dot_general | solution.py:43
  228.7 5.2 %reduce-window.36 = f32[1,16,2,2,128]{4,1,2,3,0:T(8,128)S(1)} reduce-window(f32[1,16,2,2,128]{4,1,2,3,0:T(8,128)S(1)} %copy_bitcast_fusion, f32[]{:T(128)} %constant.212.clone.1), window={size=1x1x1x1x128 pad=0_0x0_0x0_0x0_0x0_127}, to_apply=%region_21.22 | reduce-window | flops 1040384 | bytes 65540 | tf_op jit(solution)/shard_map/reduce-window.6
  234.4 5.0 %reduce-window.34 = f32[1,16,2,2,128]{4,1,2,3,0:T(8,128)S(1)} reduce-window(f32[1,16,2,2,128]{4,1,2,3,0:T(8,128)S(1)} %bitcast.270, f32[]{:T(128)} %constant.212.clone.1), window={size=1x1x1x1x128 pad=0_0x0_0x0_0x0_0x0_127}, to_apply=%region_16.17 | reduce-window | flops 1040384 | bytes 65540 | tf_op jit(solution)/shard_map/reduce-window.4
  (201 shorter events, 49.2 us)
Async XLA Ops:
  7.2 106.3 %reduce-scatter.2.cloned.1.call-start = ((), (), s32[]{:S(2)}) async-start(), calls=%async_computation.1 | async-start | bytes 9437184 | tf_op jit(solution)/shard_map/reduce_scatter | solution.py:151
  8.9 22.1 %copy-start.17 = (f32[256,32]{0,1:T(8,128)}, f32[256,32]{0,1:T(8,128)S(1)}, u32[]{:S(2)}) copy-start(f32[256,32]{0,1:T(8,128)S(1)} %compare_select_fusion) | copy-start | bytes 98308
  12.2 3.8 %copy-start.41 = (f32[256]{0:T(256)}, f32[256]{0:T(256)S(1)}, u32[]{:S(2)}) copy-start(f32[256]{0:T(256)S(1)} %get-tuple-element.377) | copy-start | bytes 3076
  15.2 15.8 %copy-start.14 = (f32[1,16,2,256]{3,1,2,0:T(8,128)}, f32[1,16,2,256]{3,1,2,0:T(8,128)S(1)}, u32[]{:S(2)}) copy-start(f32[1,16,2,256]{3,1,2,0:T(8,128)S(1)} %get-tuple-element.376) | copy-start | bytes 98308
  29.7 106.6 %copy-start = (bf16[256,2048]{0,1:T(8,128)(2,1)}, bf16[256,2048]{0,1:T(8,128)(2,1)S(1)}, u32[]{:S(2)}) copy-start(bf16[256,2048]{0,1:T(8,128)(2,1)S(1)} %copy.125) | copy-start | bytes 3145732
  41.7 152.8 %all-gather.5.cloned.1.call-start = ((), (), s32[]{:S(2)}) async-start(), calls=%async_computation.2 | async-start | bytes 9437184 | tf_op jit(solution)/shard_map/all_gather | solution.py:17
  42.4 4.3 %copy-start.9 = (bf16[256,2,128]{0,2,1:T(8,128)(2,1)}, bf16[256,2,128]{0,2,1:T(8,128)(2,1)S(1)}, u32[]{:S(2)}) copy-start(bf16[256,2,128]{0,2,1:T(8,128)(2,1)S(1)} %copy.126) | copy-start | bytes 393220
  44.0 78.2 %copy-start.3 = (bf16[256,2048]{0,1:T(8,128)(2,1)}, bf16[256,2048]{0,1:T(8,128)(2,1)S(1)}, u32[]{:S(2)}) copy-start(bf16[256,2048]{0,1:T(8,128)(2,1)S(1)} %copy.139) | copy-start | bytes 3145732
  45.8 76.3 %copy-start.4 = (bf16[256,2048]{0,1:T(8,128)(2,1)}, bf16[256,2048]{0,1:T(8,128)(2,1)S(1)}, u32[]{:S(2)}) copy-start(bf16[256,2048]{0,1:T(8,128)(2,1)S(1)} %copy.140) | copy-start | bytes 3145732
  48.8 67.0 %copy-start.15 = (f32[1,16,2,256]{3,1,2,0:T(8,128)S(1)}, f32[1,16,2,256]{3,1,2,0:T(8,128)}, u32[]{:S(2)}) copy-start(f32[1,16,2,256]{3,1,2,0:T(8,128)} %copy-done.14) | copy-start | bytes 98308
  48.8 67.0 %copy-start.18 = (f32[256,32]{0,1:T(8,128)S(1)}, f32[256,32]{0,1:T(8,128)}, u32[]{:S(2)}) copy-start(f32[256,32]{0,1:T(8,128)} %copy-done.17) | copy-start | bytes 98308
  48.8 67.0 %copy-start.23 = (f32[256,2,16]{0,2,1:T(8,128)S(1)}, f32[256,2,16]{0,2,1:T(8,128)}, u32[]{:S(2)}) copy-start(f32[256,2,16]{0,2,1:T(8,128)} %get-tuple-element.375) | copy-start | bytes 98308
  115.8 6.4 %copy-start.5 = (f32[2,16,64,256]{3,2,1,0:T(8,128)}, f32[2,16,64,256]{3,2,1,0:T(8,128)S(1)}, u32[]{:S(2)}) copy-start(f32[2,16,64,256]{3,2,1,0:T(8,128)S(1)} %fusion.81) | copy-start | bytes 6291460
  115.9 6.3 %copy-start.38 = (f32[2048]{0:T(1024)S(1)}, f32[2048]{0:T(1024)}, u32[]{:S(2)}) copy-start(f32[2048]{0:T(1024)} %param.21) | copy-start | bytes 24580
  160.0 17.9 %copy-start.28 = (f32[256,256]{1,0:T(8,128)}, f32[256,256]{1,0:T(8,128)S(1)}, u32[]{:S(2)}) copy-start(f32[256,256]{1,0:T(8,128)S(1)} %fusion.78) | copy-start | bytes 786436
  161.7 16.2 %copy-start.21 = (f32[2,256,256]{2,1,0:T(8,128)}, f32[2,256,256]{2,1,0:T(8,128)S(1)}, u32[]{:S(2)}) copy-start(f32[2,256,256]{2,1,0:T(8,128)S(1)} %fusion.105) | copy-start | bytes 1572868
  161.7 16.2 %copy-start.7 = (f32[256,2,128]{0,2,1:T(8,128)S(1)}, f32[256,2,128]{0,2,1:T(8,128)}, u32[]{:S(2)}) copy-start(f32[256,2,128]{0,2,1:T(8,128)} %squeeze.97) | copy-start | bytes 786436
  161.7 16.9 %copy-start.2 = (f32[32,64,128]{2,1,0:T(8,128)S(1)}, f32[32,64,128]{2,1,0:T(8,128)}, u32[]{:S(2)}) copy-start(f32[32,64,128]{2,1,0:T(8,128)} %reduce-scatter.2.cloned.1.call-done) | copy-start | bytes 3145732
  161.7 16.9 %copy-start.24 = (f32[256,2,16]{0,2,1:T(8,128)S(1)}, f32[256,2,16]{0,2,1:T(8,128)}, u32[]{:S(2)}) copy-start(f32[256,2,16]{0,2,1:T(8,128)} %get-tuple-element.375) | copy-start | bytes 98308
  177.9 3.5 %copy-start.8 = (f32[2,256,256]{2,1,0:T(8,128)}, f32[2,256,256]{2,1,0:T(8,128)S(1)}, u32[]{:S(2)}) copy-start(f32[2,256,256]{2,1,0:T(8,128)S(1)} %get-tuple-element.353) | copy-start | bytes 1572868
  225.9 13.9 %copy-start.37 = (f32[2,16,256]{2,1,0:T(8,128)S(1)}, f32[2,16,256]{2,1,0:T(8,128)}, u32[]{:S(2)}) copy-start(f32[2,16,256]{2,1,0:T(8,128)} %get-tuple-element.352) | copy-start | bytes 98308
  225.9 13.9 %copy-start.45 = (f32[2,16]{1,0:T(2,128)S(1)}, f32[2,16]{1,0:T(2,128)}, u32[]{:S(2)}) copy-start(f32[2,16]{1,0:T(2,128)} %copy-done.44) | copy-start | bytes 388
  225.9 14.0 %copy-start.32 = (f32[256,32]{0,1:T(8,128)S(1)}, f32[256,32]{0,1:T(8,128)}, u32[]{:S(2)}) copy-start(f32[256,32]{0,1:T(8,128)} %param.15) | copy-start | bytes 98308
  225.9 14.0 %copy-start.46 = (f32[32]{0:T(128)S(1)}, f32[32]{0:T(128)}, u32[]{:S(2)}) copy-start(f32[32]{0:T(128)} %param.18) | copy-start | bytes 388
  (26 other events, 51.7 us)
Sparse Core Ops, SparseCore 0:
  41.8 71.6 reduce-scatter.1
  142.9 51.6 all-gather.4
where the time goes:
time: 252 us; the launch traced here: 248 us
  waiting for transfers between devices  71.2 us (28%)
  other arithmetic  51.5 us (20%)
  matrix products  48.6 us (19%)
  blocking collectives  31.8 us (13%)
  local copies, waits for them, and re-layouts  27.1 us (11%)
  between operations  16.4 us (7%)
    reduce_scatter x1, waiting for transfers between devices, body(): lax.psum_scatter(weight[:, None, None] * jnp.take(flat_end, head_ids, axi...  64.7 us
    dot_general x3, matrix products, span_mix(): jnp.einsum('ghts,sghp->tghp', weights, x_span, precision=HIGHEST_PRECISION)  29.9 us
    another operation x11, other arithmetic  12.8 us
    select_n x8, other arithmetic, turn(): return jax.tree.map(lambda a, b: jnp.where(reached, a, b), new, before)  11.7 us
    psum x1, blocking collectives, body(): lax.psum((jnp.sum(gated * gated, axis=1), jnp.sum(weighted_grad * gated,...  11.7 us
    unnamed x104, local copies, waits for them, and re-layouts  10.5 us
    all_gather x1, blocking collectives, body(): lax.all_gather(through_all.reshape(1, heads_here), 'ctx', axis=0, tiled=T...  10.2 us
    all_gather x1, blocking collectives, carried_in(): everything = jax.tree.map(lambda part: lax.all_gather(part, axis), array)  9.93 us
  transfers between devices with their start and end apart: 2, of which 2 were waited for; matrix products, arithmetic and copies ran while one was open for 17% of the time, Pallas kernels for 0%

commit v1 on v0

v1 whole, which is shorter than its diff:
```python
import functools

import jax
import jax.numpy as jnp
from jax import lax
from jax.experimental import pallas as pl
from jax.experimental.pallas import tpu as pltpu
from jax.sharding import PartitionSpec as P

HEAD_DIM = 64
STATE = 128
EPSILON = 1e-05
NCH = 4
F32 = jnp.float32
BF16 = jnp.bfloat16
MESH = pl.DeviceIdType.MESH


def dot(a, b):
    return lax.dot_general(a, b, (((1,), (0,)), ((), ())), preferred_element_type=F32)


def dot_t(a, b):
    return lax.dot_general(a, b, (((1,), (1,)), ((), ())), preferred_element_type=F32)


def split(v):
    hi = v.astype(BF16)
    return hi, (v - hi.astype(F32)).astype(BF16)


def split3(v):
    hi = v.astype(BF16)
    rest = v - hi.astype(F32)
    mid = rest.astype(BF16)
    return hi, mid, (rest - mid.astype(F32)).astype(BF16)


def iota(shape, axis):
    return lax.broadcasted_iota(jnp.int32, shape, axis)


def kernel(
    n_ctx, n_head, width,
    x_ref, gate_ref, step_ref, b_ref, c_ref, bias_ref, rate_ref, skip_ref, nw_ref, reset_ref, go_ref,
    gx_ref, gg_ref, gs_ref, gb_ref, gc_ref,
    loc, cbuf, tot, rbuf, obuf, entry,
    lcrep, rrep, lct, rt, negm, negmt, smat, smatt, dst,
    ybuf, dybuf, dyh_ref, dyl_ref, edh_ref, edl_ref, xsh_ref, xsl_ref, dxbuf, tdx, eexp,
    nsend, nrecv, send_sem, recv_sem, nsend_sem, nrecv_sem,
):
    T, HP = x_ref.shape
    H = step_ref.shape[1]
    G = b_ref.shape[1] // STATE
    per = H // G
    blocks = 2 * NCH
    CH = HP // blocks
    bpg = blocks // G
    bits = n_ctx.bit_length() - 1
    me = lax.axis_index("ctx")
    me_h = lax.axis_index("head")
    core = lax.rem(me, 2)
    other = 1 - core

    def partner(j):
        bit = lax.rem(me // (1 << j), 2)
        return me + (1 - 2 * bit) * (1 << j), bit

    barrier = pltpu.get_barrier_semaphore()
    for j in range(bits):
        pl.semaphore_signal(barrier, inc=1, device_id={"ctx": partner(j)[0]}, device_id_type=MESH)
    for d in range(1, n_head):
        pl.semaphore_signal(barrier, inc=1, device_id={"head": lax.rem(me_h + d, n_head)}, device_id_type=MESH)

    shifted = step_ref[...] + bias_ref[...]
    dt = jnp.maximum(shifted, 0.0) + jnp.log1p(jnp.exp(-jnp.abs(shifted)))
    sig_step = 1.0 / (1.0 + jnp.exp(-shifted))
    rate = -jnp.exp(rate_ref[...])
    tri = (iota((T, T), 0) >= iota((T, T), 1)).astype(F32).astype(BF16)
    triu = (iota((T, T), 0) <= iota((T, T), 1)).astype(F32).astype(BF16)
    lc = sum(dot(tri, part) for part in split3(dt * rate))
    rcol = jnp.log(dt) - lc
    lc_end = lc[T - 1 : T, :]
    r8 = jnp.broadcast_to(reset_ref[...].astype(F32), (8, T)).astype(BF16)
    seg_row = dot(r8, triu)[0:1, :]
    seg_col = dot_t(tri, r8)[:, 0:1]
    seg_end = seg_row[:, T - 1 : T]
    opened = (seg_col == 0.0).astype(F32)
    same_end = (seg_col == seg_end).astype(F32)
    through = jnp.exp(lc_end) * (seg_end == 0.0).astype(F32)
    e_col = jnp.exp(lc) * opened
    taudt = jnp.exp(lc_end - lc) * same_end * dt

    eh = (iota((H, HP), 1) // HEAD_DIM == iota((H, HP), 0)).astype(F32).astype(BF16)
    wide = (iota((H, H * 128), 1) // 128 == iota((H, H * 128), 0)).astype(F32).astype(BF16)
    eye = (iota((H, H), 0) == iota((H, H), 1)).astype(F32).astype(BF16)
    through8 = jnp.broadcast_to(through, (8, H))
    thx = sum(dot(part, eh) for part in split(through8))
    tdx[...] = sum(dot(part, eh) for part in split(taudt))
    for i in range(blocks):
        loc[0, i, STATE : STATE + 8, :] = thx[:, i * CH : (i + 1) * CH]
        loc[1, i, STATE : STATE + 8, :] = thx[:, i * CH : (i + 1) * CH]

    b_t = [b_ref[:, g * STATE : (g + 1) * STATE].astype(F32).T.astype(BF16) for g in range(G)]
    for i in range(blocks):
        lanes = slice(i * CH, (i + 1) * CH)
        hi, lo = split(tdx[:, lanes] * x_ref[:, lanes].astype(F32))
        xsh_ref[:, lanes] = hi
        xsl_ref[:, lanes] = lo
        bt = b_t[i // bpg]
        loc[0, i, 0:STATE, :] = dot(bt, hi) + dot(bt, lo)

    pl.semaphore_wait(barrier, bits + n_head - 1)

    def copy_to(way, slot, k, src, dst, device):
        return pltpu.make_async_remote_copy(
            src_ref=src, dst_ref=dst,
            send_sem=send_sem.at[way, slot, k], recv_sem=recv_sem.at[way, slot, k],
            device_id=device, device_id_type=MESH,
        )

    mate, _ = partner(0)

    def core_copy(way, k):
        return copy_to(way, 0, k, loc.at[way, other * NCH + k], cbuf.at[way, k], {"ctx": mate})

    def step_copy(way, j, k):
        return copy_to(way, j, k, tot.at[way, j - 1, k], rbuf.at[way, j - 1, k], {"ctx": partner(j)[0]})

    def out_copy(way, k):
        return copy_to(way, bits, k, obuf.at[way, k], entry.at[way, core * NCH + k], {"ctx": mate})

    S = STATE

    def exchange(way, work):
        own_first = (core == 0) if way == 0 else (core == 1)
        for k in range(NCH):
            core_copy(way, k).start()
        work(0)
        early_state, early_decay = [], []
        for k in range(NCH):
            core_copy(way, k).wait_recv()
            mine = loc[way, core * NCH + k]
            got = cbuf[way, k]
            early = jnp.where(own_first, mine, got)
            late = jnp.where(own_first, got, mine)
            dl = late[S : S + 1, :]
            tot[way, 0, k, 0:S, :] = dl * early[0:S, :] + late[0:S, :]
            tot[way, 0, k, S : S + 8, :] = late[S : S + 8, :] * early[S : S + 8, :]
            step_copy(way, 1, k).start()
        prefix = [None] * NCH
        for j in range(1, bits):
            bit = partner(j)[1]
            after = (bit == 1) if way == 0 else (bit == 0)
            for k in range(NCH):
                if j == 1:
                    work(k + 1)
                step_copy(way, j, k).wait_recv()
                got = rbuf[way, j - 1, k]
                if j == 1:
                    base = jnp.where(iota((S + 8, CH), 0) < S, 0.0, 1.0)
                else:
                    base = entry[way, core * NCH + k]
                moved = base[S : S + 1, :] * got
                new = jnp.where(iota((S + 8, CH), 0) < S, moved + base, moved)
                entry[way, core * NCH + k] = jnp.where(after, new, base)
                if j < bits - 1:
                    mine = tot[way, j - 1, k]
                    early = jnp.where(after, got, mine)
                    late = jnp.where(after, mine, got)
                    dl = late[S : S + 1, :]
                    tot[way, j, k, 0:S, :] = dl * early[0:S, :] + late[0:S, :]
                    tot[way, j, k, S : S + 8, :] = late[S : S + 8, :] * early[S : S + 8, :]
                    step_copy(way, j + 1, k).start()
                else:
                    mine = loc[way, core * NCH + k]
                    theirs = cbuf[way, k]
                    early = jnp.where(own_first, mine, theirs)
                    lead = entry[way, core * NCH + k]
                    trail = early[S : S + 1, :] * lead + early
                    obuf[way, k] = jnp.where(own_first, trail, lead)
                    entry[way, core * NCH + k] = jnp.where(own_first, lead, trail)
                    out_copy(way, k).start()
        for k in range(NCH):
            out_copy(way, k).wait_recv()
        for k in range(NCH):
            core_copy(way, k).wait_send()
            for j in range(1, bits):
                step_copy(way, j, k).wait_send()
            out_copy(way, k).wait_send()

    lane = iota((T, 128), 1)
    mask_a = (lane < HEAD_DIM).astype(F32).astype(BF16)
    mask_b = (lane >= HEAD_DIM).astype(F32).astype(BF16)
    pairs = H // 2

    def prepare():
        eexp[...] = sum(dot(part, eh) for part in split(e_col))
        lcrep[...] = sum(dot(part, wide) for part in split3(lc))
        rrep[...] = sum(dot(part, wide) for part in split3(rcol))
        lct[...] = sum(dot_t(eye, part) for part in split3(lc))
        rt[...] = sum(dot_t(eye, part) for part in split3(rcol))
        ok = (iota((T, T), 0) >= iota((T, T), 1)) & (seg_col == seg_row)
        negm[...] = jnp.where(ok, 0.0, -1e30)
        okt = (iota((T, T), 0) <= iota((T, T), 1)) & (seg_col == seg_row)
        negmt[...] = jnp.where(okt, 0.0, -1e30)
        for g in range(G):
            gs = slice(g * STATE, (g + 1) * STATE)
            smat[g] = dot_t(c_ref[:, gs], b_ref[:, gs])
            smatt[g] = dot_t(b_ref[:, gs], c_ref[:, gs])
            dst[g] = jnp.zeros((T, T), F32)

    def column(ref, h):
        col = ref[:, pl.ds(pl.multiple_of(h * 128, 128), 128)]
        return jnp.concatenate([col] * (T // 128), axis=1)

    def forward_pair(j, carry):
        lanes = pl.ds(pl.multiple_of(j * 128, 128), 128)
        xp = x_ref[:, lanes]
        s = smat[(2 * j) // per]
        neg = negm[...]
        y = None
        for half, mask in ((0, mask_a), (1, mask_b)):
            h = 2 * j + half
            w = jnp.exp(column(lcrep, h) + rt[pl.ds(h, 1), :] + neg) * s
            hi, lo = split(w)
            xm = xp * mask
            part = dot(hi, xm) + dot(lo, xm)
            y = part if y is None else y + part
        ybuf[:, lanes] = y
        return carry

    def backward_pair(j, carry):
        lanes = pl.ds(pl.multiple_of(j * 128, 128), 128)
        xp = x_ref[:, lanes]
        dyh = dyh_ref[:, lanes]
        dyl = dyl_ref[:, lanes]
        g = (2 * j) // per
        s = smatt[g]
        neg = negmt[...]
        dx = None
        acc = dst[g]
        for half, mask in ((0, mask_a), (1, mask_b)):
            h = 2 * j + half
            e = jnp.exp(column(rrep, h) + lct[pl.ds(h, 1), :] + neg)
            hi, lo = split(e * s)
            dh = dyh * mask
            part = dot(hi, dh) + dot(hi, dyl * mask) + dot(lo, dh)
            dx = part if dx is None else dx + part
            xm = xp * mask
            acc = acc + (dot_t(xm, dyh) + dot_t(xm, dyl)) * e
        dst[g] = acc
        dxbuf[:, lanes] = dx
        return carry

    def slices(run):
        bounds = [pairs * k // NCH for k in range(NCH + 1)]

        def work(k):
            if k > 0:
                lax.fori_loop(bounds[k - 1], bounds[k], run, 0)

        return work

    forward_work = slices(forward_pair)

    def first_work(k):
        if k == 0:
            prepare()
        forward_work(k)

    exchange(0, first_work)

    q_sum = jnp.zeros((T, CH), F32)
    p_sum = jnp.zeros((T, CH), F32)
    for i in range(blocks):
        lanes = slice(i * CH, (i + 1) * CH)
        g = i // bpg
        cg = c_ref[:, g * STATE : (g + 1) * STATE]
        hi, lo = split(entry[0, i, 0:STATE, :])
        y = ybuf[:, lanes] + (dot(cg, hi) + dot(cg, lo)) * eexp[:, lanes]
        ybuf[:, lanes] = y
        core_out = y + x_ref[:, lanes].astype(F32) * skip_ref[:, lanes]
        gate = gate_ref[:, lanes].astype(F32)
        gated = core_out * gate / (1.0 + jnp.exp(-gate))
        q_sum = q_sum + gated * gated
        p_sum = p_sum + gated * (nw_ref[:, lanes] * go_ref[:, lanes].astype(F32))
    ones8 = jnp.ones((8, CH), BF16)
    nsend[0:8, :] = sum(dot_t(ones8, part) for part in split3(q_sum))
    nsend[8:16, :] = sum(dot_t(ones8, part) for part in split3(p_sum))

    def norm_copy(d):
        return pltpu.make_async_remote_copy(
            src_ref=nsend, dst_ref=nrecv.at[d - 1],
            send_sem=nsend_sem.at[d - 1], recv_sem=nrecv_sem.at[d - 1],
            device_id={"head": lax.rem(me_h + d, n_head)}, device_id_type=MESH,
        )

    for d in range(1, n_head):
        norm_copy(d).start()
    c_t = [c_ref[:, g * STATE : (g + 1) * STATE].astype(F32).T.astype(BF16) for g in range(G)]
    sums = nsend[...]
    for d in range(1, n_head):
        norm_copy(d).wait_recv()
        sums = sums + nrecv[d - 1]
    inv_row = lax.rsqrt(sums[0:1, :] / width + EPSILON)
    coef_row = inv_row * inv_row * inv_row * sums[8:9, :] / width
    inv = jnp.broadcast_to(inv_row, (128, T)).T
    coef = jnp.broadcast_to(coef_row, (128, T)).T
    if CH > 128:
        inv = jnp.concatenate([inv] * (CH // 128), axis=1)
        coef = jnp.concatenate([coef] * (CH // 128), axis=1)

    dyy = jnp.zeros((T, H), F32)
    for i in range(blocks):
        lanes = slice(i * CH, (i + 1) * CH)
        g = i // bpg
        y = ybuf[:, lanes]
        core_out = y + x_ref[:, lanes].astype(F32) * skip_ref[:, lanes]
        gate = gate_ref[:, lanes].astype(F32)
        sig = 1.0 / (1.0 + jnp.exp(-gate))
        act = gate * sig
        weighted = nw_ref[:, lanes] * go_ref[:, lanes].astype(F32)
        ggated = inv * weighted - core_out * act * coef
        dy = ggated * act
        gg_ref[:, lanes] = (ggated * core_out * sig * (1.0 + gate * (1.0 - sig))).astype(BF16)
        dybuf[:, lanes] = dy
        dyh_ref[:, lanes], dyl_ref[:, lanes] = split(dy)
        hi, lo = split(dy * eexp[:, lanes])
        edh_ref[:, lanes] = hi
        edl_ref[:, lanes] = lo
        loc[1, i, 0:STATE, :] = dot(c_t[g], hi) + dot(c_t[g], lo)
        dyy = dyy + sum(dot_t(part, eh[:, lanes]) for part in split(dy * y))

    backward_work = slices(backward_pair)
    exchange(1, backward_work)

    for g in range(G):
        gs = slice(g * STATE, (g + 1) * STATE)
        acc = dst[g]
        hi, lo = split(acc)
        cg = c_ref[:, gs]
        gb = dot(hi, cg) + dot(lo, cg)
        hi, lo = split(acc.T)
        bg = b_ref[:, gs]
        gc = dot(hi, bg) + dot(lo, bg)
        for i in range(g * bpg, (g + 1) * bpg):
            lanes = slice(i * CH, (i + 1) * CH)
            hi, lo = split(entry[0, i, 0:STATE, :])
            edh = edh_ref[:, lanes]
            gc = gc + dot_t(edh, hi) + dot_t(edh, lo) + dot_t(edl_ref[:, lanes], hi)
            hi, lo = split(entry[1, i, 0:STATE, :])
            xsh = xsh_ref[:, lanes]
            gb = gb + dot_t(xsh, hi) + dot_t(xsh, lo) + dot_t(xsl_ref[:, lanes], hi)
        gb_ref[:, gs] = gb
        gc_ref[:, gs] = gc

    xdx = jnp.zeros((T, H), F32)
    ends = jnp.zeros((8, H), F32)
    for i in range(blocks):
        lanes = slice(i * CH, (i + 1) * CH)
        g = i // bpg
        bg = b_ref[:, g * STATE : (g + 1) * STATE]
        adj = entry[1, i, 0:STATE, :]
        hi, lo = split(adj)
        dx = dxbuf[:, lanes] + (dot(bg, hi) + dot(bg, lo)) * tdx[:, lanes]
        gx_ref[:, lanes] = (dx + dybuf[:, lanes] * skip_ref[:, lanes]).astype(BF16)
        xdx = xdx + sum(dot_t(part, eh[:, lanes]) for part in split(dx * x_ref[:, lanes].astype(F32)))
        local = loc[0, i]
        leaving = local[S : S + 1, :] * entry[0, i, 0:STATE, :] + local[0:S, :]
        col = jnp.sum(adj * leaving, axis=0, keepdims=True)
        col = jnp.broadcast_to(col, (8, CH))
        ends = ends + sum(dot_t(part, eh[:, lanes]) for part in split3(col))
    rc = sum(dot(triu, part) for part in split3(dyy - xdx)) + ends[0:1, :]
    gs_ref[...] = (xdx / dt + rate * rc) * sig_step

    for d in range(1, n_head):
        norm_copy(d).wait_send()


def body(mesh_shape, x, gate, step, b, c, bias, rate, skip, nw, resets, go):
    n_ctx, n_head = mesh_shape
    T, HP = x.shape
    H = step.shape[1]
    G = b.shape[1] // STATE
    bits = n_ctx.bit_length() - 1
    CH = HP // (2 * NCH)
    R = STATE + 8
    vm = pltpu.VMEM
    skip_cols = jnp.repeat(skip, HEAD_DIM)[None, :]
    return pl.pallas_call(
        functools.partial(kernel, n_ctx, n_head, HP * n_head),
        out_shape=(
            jax.ShapeDtypeStruct((T, HP), BF16),
            jax.ShapeDtypeStruct((T, HP), BF16),
            jax.ShapeDtypeStruct((T, H), F32),
            jax.ShapeDtypeStruct((T, G * STATE), F32),
            jax.ShapeDtypeStruct((T, G * STATE), F32),
        ),
        in_specs=[pl.BlockSpec(memory_space=pltpu.VMEM)] * 11,
        out_specs=[pl.BlockSpec(memory_space=pltpu.VMEM)] * 5,
        scratch_shapes=[
            vm((2, 2 * NCH, R, CH), F32),
            vm((2, NCH, R, CH), F32),
            vm((2, bits - 1, NCH, R, CH), F32),
            vm((2, bits - 1, NCH, R, CH), F32),
            vm((2, NCH, R, CH), F32),
            vm((2, 2 * NCH, R, CH), F32),
            vm((T, H * 128), F32),
            vm((T, H * 128), F32),
            vm((H, T), F32),
            vm((H, T), F32),
            vm((T, T), F32),
            vm((T, T), F32),
            vm((G, T, T), F32),
            vm((G, T, T), F32),
            vm((G, T, T), F32),
            vm((T, HP), F32),
            vm((T, HP), F32),
            vm((T, HP), BF16),
            vm((T, HP), BF16),
            vm((T, HP), BF16),
            vm((T, HP), BF16),
            vm((T, HP), BF16),
            vm((T, HP), BF16),
            vm((T, HP), F32),
            vm((T, HP), F32),
            vm((T, HP), F32),
            vm((16, T), F32),
            vm((max(n_head - 1, 1), 16, T), F32),
            pltpu.SemaphoreType.DMA((2, bits + 1, NCH)),
            pltpu.SemaphoreType.DMA((2, bits + 1, NCH)),
            pltpu.SemaphoreType.DMA((max(n_head - 1, 1),)),
            pltpu.SemaphoreType.DMA((max(n_head - 1, 1),)),
        ],
        compiler_params=pltpu.CompilerParams(
            collective_id=0, has_side_effects=True, vmem_limit_bytes=60 * 1024 * 1024
        ),
    )(
        x, gate, step, b, c, bias[None, :], rate[None, :], skip_cols, nw[None, :], resets[None, :], go
    )


def solution(mesh):
    return jax.shard_map(
        functools.partial(body, (mesh.shape["ctx"], mesh.shape["head"])),
        mesh=mesh,
        in_specs=(
            P("ctx", "head"), P("ctx", "head"), P("ctx", "head"), P("ctx", "head"), P("ctx", "head"),
            P("head"), P("head"), P("head"), P("head"), P("ctx"), P("ctx", "head"),
        ),
        out_specs=(P("ctx", "head"),) * 5,
        check_vma=False,
    )
```

time: 252 us -> 76.2 us (0.30); the launches traced: 248 us -> 75.9 us
  waiting for transfers between devices: 71.2 us -> 0 us
  Pallas kernels: 0 us -> 66.3 us
  other arithmetic: 51.5 us -> 0 us
  matrix products: 48.6 us -> 0 us
  blocking collectives: 31.8 us -> 0 us
  local copies, waits for them, and re-layouts: 27.1 us -> 9 us
  between operations: 16.4 us -> 0.66 us
    pallas_call x0 -> x1, Pallas kernels: none -> 66.3 us  [body(): pl.pallas_call(functools.partial(kernel, n_ctx, n_head, HP * n_head), out...]
    reduce_scatter x1 -> x0, waiting for transfers between devices: 64.7 us -> none  [body(): lax.psum_scatter(weight[:, None, None] * jnp.take(flat_end, head_ids, axi...]
    dot_general x13 -> x0, matrix products: 48.6 us -> none  [the longest x3 29.9 us: span_mix(): jnp.einsum('ghts,sghp->tghp', weights, x_span, precision=HIGHEST_PRECISION)]
    all_gather x2 -> x0, blocking collectives: 20.1 us -> none  [the longest x1 10.2 us: body(): lax.all_gather(through_all.reshape(1, heads_here), 'ctx', axis=0, tiled=T...]
    another operation x11 -> x0, other arithmetic: 12.8 us -> none
    select_n x11 -> x0, other arithmetic: 12.5 us -> none  [the longest x8 11.7 us: turn(): return jax.tree.map(lambda a, b: jnp.where(reached, a, b), new, before)]
    psum x1 -> x0, blocking collectives: 11.7 us -> none  [body(): lax.psum((jnp.sum(gated * gated, axis=1), jnp.sum(weighted_grad * gated,...]
    mul x7 -> x0, other arithmetic: 8.29 us -> none  [the longest x1 6.18 us: body(): weight[:, None, None] * jnp.take(flat_end, head_ids, axis=0)]
  transfers between devices with their start and end apart: 2 -> 0, of which waited for: 2 -> 0; matrix products, arithmetic and copies ran while one was open for 17% -> 0% of each run, Pallas kernels for 0% -> 0%
where the time goes in v1:
time: 76.2 us; the launch traced here: 75.9 us
  Pallas kernels  66.3 us (87%)
  local copies, waits for them, and re-layouts  9 us (12%)
    pallas_call x1, Pallas kernels, body(): pl.pallas_call(functools.partial(kernel, n_ctx, n_head, HP * n_head), out...  66.3 us
    unnamed x13, local copies, waits for them, and re-layouts  5.99 us
    pallas_call x1, local copies, waits for them, and re-layouts, body(): pl.pallas_call(functools.partial(kernel, n_ctx, n_head, HP * n_head), out...  1.59 us

profile of v1, /device:TPU:0, one launch (start us, length us, event | category | flops | bytes accessed | tf_op | source)
XLA Modules:
  0.0 75.9 jit_solution(12046119781958870236)
XLA Ops:
  0.6 0.0 copy-start.3
  0.6 0.7 broadcast_in_dim.17
  1.4 0.7 broadcast_in_dim_reshape.3.skip_ref
  2.1 0.0 copy-done.3
  2.1 0.8 copy.16.step_ref
  2.8 66.3 %shard_map.146 = (bf16[256,2048]{1,0:T(8,128)(2,1)}, bf16[256,2048]{1,0:T(8,128)(2,1)}, f32[256,32]{1,0:T(8,128)}, f32[256,256]{1,0:T(8,128)}, f32[256,256]{1,0:T(8,128)}) custom-call(bf16[256,2048]{1,0:T(8,128)(2,1)} %x_ref.1, bf16[256,2048]{1,0:T(8,128)(2,1)} %gate_ref.1, f32[256,32]{1,0:T(8,128)} %copy.16.step_ref, bf16[256,256]{1,0:T(8,128)(2,1)} %b_ref.1, ...), custom_call_target="tpu_custom_call" | custom-call | tf_op jit(solution)/shard_map/pallas_call | solution.py:391
  69.1 1.6 %copy.17 = f32[256,32]{0,1:T(8,128)} copy(f32[256,32]{1,0:T(8,128)} %get-tuple-element.7) | data formatting | bytes 65536 | tf_op jit(solution)/shard_map/pallas_call | solution.py:391
  70.7 0.0 copy-start
  70.7 2.4 %copy.22 = bf16[256,2048]{1,0:T(8,128)(2,1)} copy(bf16[256,2048]{1,0:T(8,128)(2,1)} %get-tuple-element.15) | data formatting | bytes 2097152
  73.1 0.0 copy-done
  73.1 0.0 copy-start.2
  73.1 1.0 %copy.23 = bf16[256,2048]{1,0:T(8,128)(2,1)} copy(bf16[256,2048]{1,0:T(8,128)(2,1)S(1)} %copy-done) | data formatting | bytes 2097152
  74.1 0.1 copy-done.2
  74.2 0.0 copy-start.1
  74.2 0.7 copy.24
  74.9 0.3 copy-done.1
  75.2 0.7 copy.25
Async XLA Ops:
  0.6 1.4 %copy-start.3 = (f32[256,32]{0,1:T(8,128)S(1)}, f32[256,32]{0,1:T(8,128)}, u32[]{:S(2)}) copy-start(f32[256,32]{0,1:T(8,128)} %param.13) | copy-start | bytes 98308
  70.7 2.4 %copy-start = (bf16[256,2048]{1,0:T(8,128)(2,1)S(1)}, bf16[256,2048]{1,0:T(8,128)(2,1)}, u32[]{:S(2)}) copy-start(bf16[256,2048]{1,0:T(8,128)(2,1)} %get-tuple-element.16) | copy-start | bytes 3145732
  73.1 1.1 %copy-start.2 = (f32[256,256]{1,0:T(8,128)S(1)}, f32[256,256]{1,0:T(8,128)}, u32[]{:S(2)}) copy-start(f32[256,256]{1,0:T(8,128)} %get-tuple-element.18) | copy-start | bytes 786436
  74.2 1.0 %copy-start.1 = (f32[256,256]{1,0:T(8,128)S(1)}, f32[256,256]{1,0:T(8,128)}, u32[]{:S(2)}) copy-start(f32[256,256]{1,0:T(8,128)} %get-tuple-element.19) | copy-start | bytes 786436

commit v2 on v1

--- a/solution.py
+++ b/solution.py
@@ -47,7 +47,7 @@
     loc, cbuf, tot, rbuf, obuf, entry,
     lcrep, rrep, lct, rt, negm, negmt, smat, smatt, dst,
     ybuf, dybuf, dyh_ref, dyl_ref, edh_ref, edl_ref, xsh_ref, xsl_ref, dxbuf, tdx, eexp,
-    nsend, nrecv, send_sem, recv_sem, nsend_sem, nrecv_sem,
+    btr, ctr, actb, wb, qacc, pacc, dyya, xdxa, nsend, nrecv, send_sem, recv_sem, nsend_sem, nrecv_sem,
 ):
     T, HP = x_ref.shape
     H = step_ref.shape[1]
@@ -101,13 +101,27 @@
         loc[0, i, STATE : STATE + 8, :] = thx[:, i * CH : (i + 1) * CH]
         loc[1, i, STATE : STATE + 8, :] = thx[:, i * CH : (i + 1) * CH]
 
-    b_t = [b_ref[:, g * STATE : (g + 1) * STATE].astype(F32).T.astype(BF16) for g in range(G)]
-    for i in range(blocks):
-        lanes = slice(i * CH, (i + 1) * CH)
+    for g in range(G):
+        gs = slice(g * STATE, (g + 1) * STATE)
+        btr[g] = b_ref[:, gs].astype(F32).T.astype(BF16)
+        ctr[g] = c_ref[:, gs].astype(F32).T.astype(BF16)
+
+    def lanes_of(i):
+        return pl.ds(pl.multiple_of(i * CH, CH), CH)
+
+    def group_of(i):
+        return pl.ds(pl.multiple_of((i // bpg) * STATE, STATE), STATE)
+
+    def heads_of(i):
+        first = i * (CH // HEAD_DIM)
+        return (iota((H, CH), 1) // HEAD_DIM + first == iota((H, CH), 0)).astype(F32).astype(BF16)
+
+    def local_state(i):
+        lanes = lanes_of(i)
         hi, lo = split(tdx[:, lanes] * x_ref[:, lanes].astype(F32))
         xsh_ref[:, lanes] = hi
         xsl_ref[:, lanes] = lo
-        bt = b_t[i // bpg]
+        bt = btr[i // bpg]
         loc[0, i, 0:STATE, :] = dot(bt, hi) + dot(bt, lo)
 
     pl.semaphore_wait(barrier, bits + n_head - 1)
@@ -132,12 +146,13 @@
 
     S = STATE
 
-    def exchange(way, work):
+    def exchange(way, produce, work, done):
         own_first = (core == 0) if way == 0 else (core == 1)
         for k in range(NCH):
+            produce(other * NCH + k)
             core_copy(way, k).start()
-        work(0)
-        early_state, early_decay = [], []
+        for k in range(NCH):
+            produce(core * NCH + k)
         for k in range(NCH):
             core_copy(way, k).wait_recv()
             mine = loc[way, core * NCH + k]
@@ -148,13 +163,11 @@
             tot[way, 0, k, 0:S, :] = dl * early[0:S, :] + late[0:S, :]
             tot[way, 0, k, S : S + 8, :] = late[S : S + 8, :] * early[S : S + 8, :]
             step_copy(way, 1, k).start()
-        prefix = [None] * NCH
+        work(0)
         for j in range(1, bits):
             bit = partner(j)[1]
             after = (bit == 1) if way == 0 else (bit == 0)
             for k in range(NCH):
-                if j == 1:
-                    work(k + 1)
                 step_copy(way, j, k).wait_recv()
                 got = rbuf[way, j - 1, k]
                 if j == 1:
@@ -172,6 +185,8 @@
                     tot[way, j, k, 0:S, :] = dl * early[0:S, :] + late[0:S, :]
                     tot[way, j, k, S : S + 8, :] = late[S : S + 8, :] * early[S : S + 8, :]
                     step_copy(way, j + 1, k).start()
+                    if j == 1:
+                        work(k + 1)
                 else:
                     mine = loc[way, core * NCH + k]
                     theirs = cbuf[way, k]
@@ -181,8 +196,12 @@
                     obuf[way, k] = jnp.where(own_first, trail, lead)
                     entry[way, core * NCH + k] = jnp.where(own_first, lead, trail)
                     out_copy(way, k).start()
+                    done(core * NCH + k)
+            if j == 1:
+                work(NCH + 1)
         for k in range(NCH):
             out_copy(way, k).wait_recv()
+            done(other * NCH + k)
         for k in range(NCH):
             core_copy(way, k).wait_send()
             for j in range(1, bits):
@@ -257,7 +276,7 @@
         bounds = [pairs * k // NCH for k in range(NCH + 1)]
 
         def work(k):
-            if k > 0:
+            if 0 < k <= NCH:
                 lax.fori_loop(bounds[k - 1], bounds[k], run, 0)
 
         return work
@@ -268,23 +287,30 @@
         if k == 0:
             prepare()
         forward_work(k)
-
-    exchange(0, first_work)
-
-    q_sum = jnp.zeros((T, CH), F32)
-    p_sum = jnp.zeros((T, CH), F32)
-    for i in range(blocks):
-        lanes = slice(i * CH, (i + 1) * CH)
-        g = i // bpg
-        cg = c_ref[:, g * STATE : (g + 1) * STATE]
+        if 0 < k <= NCH:
+            for i in (2 * k - 2, 2 * k - 1):
+                lanes = lanes_of(i)
+                gate = gate_ref[:, lanes].astype(F32)
+                actb[:, lanes] = gate / (1.0 + jnp.exp(-gate))
+                wb[:, lanes] = nw_ref[:, lanes] * go_ref[:, lanes].astype(F32)
+
+    qacc[...] = jnp.zeros((T, CH), F32)
+    pacc[...] = jnp.zeros((T, CH), F32)
+
+    def gate_block(i):
+        lanes = lanes_of(i)
+        cg = c_ref[:, group_of(i)]
         hi, lo = split(entry[0, i, 0:STATE, :])
         y = ybuf[:, lanes] + (dot(cg, hi) + dot(cg, lo)) * eexp[:, lanes]
         ybuf[:, lanes] = y
-        core_out = y + x_ref[:, lanes].astype(F32) * skip_ref[:, lanes]
-        gate = gate_ref[:, lanes].astype(F32)
-        gated = core_out * gate / (1.0 + jnp.exp(-gate))
-        q_sum = q_sum + gated * gated
-        p_sum = p_sum + gated * (nw_ref[:, lanes] * go_ref[:, lanes].astype(F32))
+        gated = (y + x_ref[:, lanes].astype(F32) * skip_ref[:, lanes]) * actb[:, lanes]
+        qacc[...] += gated * gated
+        pacc[...] += gated * wb[:, lanes]
+
+    exchange(0, local_state, first_work, gate_block)
+
+    q_sum = qacc[...]
+    p_sum = pacc[...]
     ones8 = jnp.ones((8, CH), BF16)
     nsend[0:8, :] = sum(dot_t(ones8, part) for part in split3(q_sum))
     nsend[8:16, :] = sum(dot_t(ones8, part) for part in split3(p_sum))
@@ -298,7 +324,6 @@
 
     for d in range(1, n_head):
         norm_copy(d).start()
-    c_t = [c_ref[:, g * STATE : (g + 1) * STATE].astype(F32).T.astype(BF16) for g in range(G)]
     sums = nsend[...]
     for d in range(1, n_head):
         norm_copy(d).wait_recv()
@@ -311,66 +336,81 @@
         inv = jnp.concatenate([inv] * (CH // 128), axis=1)
         coef = jnp.concatenate([coef] * (CH // 128), axis=1)
 
-    dyy = jnp.zeros((T, H), F32)
-    for i in range(blocks):
-        lanes = slice(i * CH, (i + 1) * CH)
-        g = i // bpg
-        y = ybuf[:, lanes]
-        core_out = y + x_ref[:, lanes].astype(F32) * skip_ref[:, lanes]
-        gate = gate_ref[:, lanes].astype(F32)
-        sig = 1.0 / (1.0 + jnp.exp(-gate))
-        act = gate * sig
-        weighted = nw_ref[:, lanes] * go_ref[:, lanes].astype(F32)
-        ggated = inv * weighted - core_out * act * coef
-        dy = ggated * act
-        gg_ref[:, lanes] = (ggated * core_out * sig * (1.0 + gate * (1.0 - sig))).astype(BF16)
+    def adjoint_block(i):
+        lanes = lanes_of(i)
+        act = actb[:, lanes]
+        gated = (ybuf[:, lanes] + x_ref[:, lanes].astype(F32) * skip_ref[:, lanes]) * act
+        dy = (inv * wb[:, lanes] - gated * coef) * act
         dybuf[:, lanes] = dy
         dyh_ref[:, lanes], dyl_ref[:, lanes] = split(dy)
         hi, lo = split(dy * eexp[:, lanes])
         edh_ref[:, lanes] = hi
         edl_ref[:, lanes] = lo
-        loc[1, i, 0:STATE, :] = dot(c_t[g], hi) + dot(c_t[g], lo)
-        dyy = dyy + sum(dot_t(part, eh[:, lanes]) for part in split(dy * y))
+        ct = ctr[i // bpg]
+        loc[1, i, 0:STATE, :] = dot(ct, hi) + dot(ct, lo)
+
+    dyya[...] = jnp.zeros((T, H), F32)
+    xdxa[...] = jnp.zeros((T, H), F32)
+
+    def gate_grad(i):
+        lanes = lanes_of(i)
+        y = ybuf[:, lanes]
+        core_out = y + x_ref[:, lanes].astype(F32) * skip_ref[:, lanes]
+        gate = gate_ref[:, lanes].astype(F32)
+        sig = 1.0 / (1.0 + jnp.exp(-gate))
+        ggated = inv * wb[:, lanes] - core_out * actb[:, lanes] * coef
+        gg_ref[:, lanes] = (ggated * core_out * sig * (1.0 + gate * (1.0 - sig))).astype(BF16)
+        dyya[...] += sum(dot_t(part, heads_of(i)) for part in split(dybuf[:, lanes] * y))
 
     backward_work = slices(backward_pair)
-    exchange(1, backward_work)
-
-    for g in range(G):
-        gs = slice(g * STATE, (g + 1) * STATE)
-        acc = dst[g]
-        hi, lo = split(acc)
-        cg = c_ref[:, gs]
-        gb = dot(hi, cg) + dot(lo, cg)
-        hi, lo = split(acc.T)
+
+    def second_work(k):
+        backward_work(k)
+        if k == 0:
+            for i in range(NCH):
+                gate_grad(i)
+        elif k <= NCH:
+            gate_grad(NCH + k - 1)
+        else:
+            for g in range(G):
+                gs = slice(g * STATE, (g + 1) * STATE)
+                acc = dst[g]
+                hi, lo = split(acc)
+                cg = c_ref[:, gs]
+                gb_ref[:, gs] = dot(hi, cg) + dot(lo, cg)
+                hi, lo = split(acc.T)
+                bg = b_ref[:, gs]
+                gc = dot(hi, bg) + dot(lo, bg)
+                for i in range(g * bpg, (g + 1) * bpg):
+                    lanes = lanes_of(i)
+                    hi, lo = split(entry[0, i, 0:STATE, :])
+                    edh = edh_ref[:, lanes]
+                    gc = gc + dot_t(edh, hi) + dot_t(edh, lo) + dot_t(edl_ref[:, lanes], hi)
+                gc_ref[:, gs] = gc
+
+    ends_of = []
+
+    def input_block(i):
+        lanes = lanes_of(i)
+        gs = group_of(i)
         bg = b_ref[:, gs]
-        gc = dot(hi, bg) + dot(lo, bg)
-        for i in range(g * bpg, (g + 1) * bpg):
-            lanes = slice(i * CH, (i + 1) * CH)
-            hi, lo = split(entry[0, i, 0:STATE, :])
-            edh = edh_ref[:, lanes]
-            gc = gc + dot_t(edh, hi) + dot_t(edh, lo) + dot_t(edl_ref[:, lanes], hi)
-            hi, lo = split(entry[1, i, 0:STATE, :])
-            xsh = xsh_ref[:, lanes]
-            gb = gb + dot_t(xsh, hi) + dot_t(xsh, lo) + dot_t(xsl_ref[:, lanes], hi)
-        gb_ref[:, gs] = gb
-        gc_ref[:, gs] = gc
-
-    xdx = jnp.zeros((T, H), F32)
-    ends = jnp.zeros((8, H), F32)
-    for i in range(blocks):
-        lanes = slice(i * CH, (i + 1) * CH)
-        g = i // bpg
-        bg = b_ref[:, g * STATE : (g + 1) * STATE]
         adj = entry[1, i, 0:STATE, :]
         hi, lo = split(adj)
+        xsh = xsh_ref[:, lanes]
+        gb_ref[:, gs] += dot_t(xsh, hi) + dot_t(xsh, lo) + dot_t(xsl_ref[:, lanes], hi)
         dx = dxbuf[:, lanes] + (dot(bg, hi) + dot(bg, lo)) * tdx[:, lanes]
         gx_ref[:, lanes] = (dx + dybuf[:, lanes] * skip_ref[:, lanes]).astype(BF16)
-        xdx = xdx + sum(dot_t(part, eh[:, lanes]) for part in split(dx * x_ref[:, lanes].astype(F32)))
+        eb = heads_of(i)
+        xdxa[...] += sum(dot_t(part, eb) for part in split(dx * x_ref[:, lanes].astype(F32)))
         local = loc[0, i]
         leaving = local[S : S + 1, :] * entry[0, i, 0:STATE, :] + local[0:S, :]
-        col = jnp.sum(adj * leaving, axis=0, keepdims=True)
-        col = jnp.broadcast_to(col, (8, CH))
-        ends = ends + sum(dot_t(part, eh[:, lanes]) for part in split3(col))
+        col = jnp.broadcast_to(jnp.sum(adj * leaving, axis=0, keepdims=True), (8, CH))
+        ends_of.append(sum(dot_t(part, eb) for part in split3(col)))
+
+    exchange(1, adjoint_block, second_work, input_block)
+    ends = sum(ends_of)
+    xdx = xdxa[...]
+    dyy = dyya[...]
     rc = sum(dot(triu, part) for part in split3(dyy - xdx)) + ends[0:1, :]
     gs_ref[...] = (xdx / dt + rate * rc) * sig_step
 
@@ -426,6 +466,14 @@
             vm((T, HP), F32),
             vm((T, HP), F32),
             vm((T, HP), F32),
+            vm((G, STATE, T), BF16),
+            vm((G, STATE, T), BF16),
+            vm((T, HP), F32),
+            vm((T, HP), F32),
+            vm((T, CH), F32),
+            vm((T, CH), F32),
+            vm((T, H), F32),
+            vm((T, H), F32),
             vm((16, T), F32),
             vm((max(n_head - 1, 1), 16, T), F32),
             pltpu.SemaphoreType.DMA((2, bits + 1, NCH)),

time: 76.2 us -> 71.6 us (0.940)
  Pallas kernels: 66.3 us -> 61.6 us
    pallas_call x1, Pallas kernels: 66.3 us -> 61.6 us  [body(): pl.pallas_call(functools.partial(kernel, n_ctx, n_head, HP * n_head), out...]
where the time goes in v2:
time: 71.6 us; the launch traced here: 71.3 us
  Pallas kernels  61.6 us (86%)
  local copies, waits for them, and re-layouts  9 us (13%)
    pallas_call x1, Pallas kernels, body(): pl.pallas_call(functools.partial(kernel, n_ctx, n_head, HP * n_head), out...  61.6 us
    unnamed x13, local copies, waits for them, and re-layouts  5.99 us
    pallas_call x1, local copies, waits for them, and re-layouts, body(): pl.pallas_call(functools.partial(kernel, n_ctx, n_head, HP * n_head), out...  1.59 us

profile of v2, /device:TPU:0, one launch (start us, length us, event | category | flops | bytes accessed | tf_op | source)
XLA Modules:
  0.0 71.3 jit_solution(2679058884923376934)
XLA Ops:
  0.6 0.0 copy-start.3
  0.6 0.7 %broadcast_in_dim.17 = f32[32,64]{1,0:T(8,128)S(1)} broadcast(f32[32]{0:T(128)} %param.18), dimensions={0} | broadcast | bytes 8320 | tf_op jit(solution)/shard_map/broadcast_in_dim | solution.py:430
  1.4 0.7 broadcast_in_dim_reshape.3.skip_ref
  2.1 0.0 copy-done.3
  2.1 0.8 %copy.16.step_ref = f32[256,32]{1,0:T(8,128)} copy(f32[256,32]{0,1:T(8,128)S(1)} %copy-done.3) | data formatting | bytes 65536 | tf_op args[2]
  2.8 61.6 %shard_map.146 = (bf16[256,2048]{1,0:T(8,128)(2,1)}, bf16[256,2048]{1,0:T(8,128)(2,1)}, f32[256,32]{1,0:T(8,128)}, f32[256,256]{1,0:T(8,128)}, f32[256,256]{1,0:T(8,128)}) custom-call(bf16[256,2048]{1,0:T(8,128)(2,1)} %x_ref.1, bf16[256,2048]{1,0:T(8,128)(2,1)} %gate_ref.1, f32[256,32]{1,0:T(8,128)} %copy.16.step_ref, bf16[256,256]{1,0:T(8,128)(2,1)} %b_ref.1, ...), custom_call_target="tpu_custom_call" | custom-call | tf_op jit(solution)/shard_map/pallas_call | solution.py:431
  64.5 1.6 %copy.17 = f32[256,32]{0,1:T(8,128)} copy(f32[256,32]{1,0:T(8,128)} %get-tuple-element.7) | data formatting | bytes 65536 | tf_op jit(solution)/shard_map/pallas_call | solution.py:431
  66.1 0.0 copy-start
  66.1 2.4 %copy.22 = bf16[256,2048]{1,0:T(8,128)(2,1)} copy(bf16[256,2048]{1,0:T(8,128)(2,1)} %get-tuple-element.15) | data formatting | bytes 2097152
  68.4 0.0 copy-done
  68.5 0.0 copy-start.2
  68.5 1.0 %copy.23 = bf16[256,2048]{1,0:T(8,128)(2,1)} copy(bf16[256,2048]{1,0:T(8,128)(2,1)S(1)} %copy-done) | data formatting | bytes 2097152
  69.4 0.1 copy-done.2
  69.5 0.0 copy-start.1
  69.5 0.7 copy.24
  70.2 0.3 copy-done.1
  70.6 0.7 copy.25
Async XLA Ops:
  0.6 1.4 %copy-start.3 = (f32[256,32]{0,1:T(8,128)S(1)}, f32[256,32]{0,1:T(8,128)}, u32[]{:S(2)}) copy-start(f32[256,32]{0,1:T(8,128)} %param.13) | copy-start | bytes 98308
  66.1 2.4 %copy-start = (bf16[256,2048]{1,0:T(8,128)(2,1)S(1)}, bf16[256,2048]{1,0:T(8,128)(2,1)}, u32[]{:S(2)}) copy-start(bf16[256,2048]{1,0:T(8,128)(2,1)} %get-tuple-element.16) | copy-start | bytes 3145732
  68.5 1.1 %copy-start.2 = (f32[256,256]{1,0:T(8,128)S(1)}, f32[256,256]{1,0:T(8,128)}, u32[]{:S(2)}) copy-start(f32[256,256]{1,0:T(8,128)} %get-tuple-element.18) | copy-start | bytes 786436
  69.5 1.0 %copy-start.1 = (f32[256,256]{1,0:T(8,128)S(1)}, f32[256,256]{1,0:T(8,128)}, u32[]{:S(2)}) copy-start(f32[256,256]{1,0:T(8,128)} %get-tuple-element.19) | copy-start | bytes 786436

commit v3 on v2

--- a/solution.py
+++ b/solution.py
@@ -153,7 +153,6 @@
             core_copy(way, k).start()
         for k in range(NCH):
             produce(core * NCH + k)
-        for k in range(NCH):
             core_copy(way, k).wait_recv()
             mine = loc[way, core * NCH + k]
             got = cbuf[way, k]
@@ -367,11 +366,13 @@
     def second_work(k):
         backward_work(k)
         if k == 0:
-            for i in range(NCH):
+            for i in range(NCH // 2):
                 gate_grad(i)
         elif k <= NCH:
-            gate_grad(NCH + k - 1)
+            gate_grad(NCH // 2 + k - 1)
         else:
+            for i in range(NCH + NCH // 2, 2 * NCH):
+                gate_grad(i)
             for g in range(G):
                 gs = slice(g * STATE, (g + 1) * STATE)
                 acc = dst[g]

time: 71.6 us -> 71.6 us (level)
  no operation moved by 1% of the time
where the time goes in v3:
time: 71.6 us; the launch traced here: 71.3 us
  Pallas kernels  61.6 us (86%)
  local copies, waits for them, and re-layouts  9 us (13%)
    pallas_call x1, Pallas kernels, body(): pl.pallas_call(functools.partial(kernel, n_ctx, n_head, HP * n_head), out...  61.6 us
    unnamed x13, local copies, waits for them, and re-layouts  5.99 us
    pallas_call x1, local copies, waits for them, and re-layouts, body(): pl.pallas_call(functools.partial(kernel, n_ctx, n_head, HP * n_head), out...  1.59 us

profile of v3, /device:TPU:0, one launch (start us, length us, event | category | flops | bytes accessed | tf_op | source)
XLA Modules:
  0.0 71.3 jit_solution(11344031159023436308)
XLA Ops:
  0.6 0.0 copy-start.3
  0.6 0.7 %broadcast_in_dim.17 = f32[32,64]{1,0:T(8,128)S(1)} broadcast(f32[32]{0:T(128)} %param.18), dimensions={0} | broadcast | bytes 8320 | tf_op jit(solution)/shard_map/broadcast_in_dim | solution.py:431
  1.4 0.7 broadcast_in_dim_reshape.3.skip_ref
  2.1 0.0 copy-done.3
  2.1 0.8 %copy.16.step_ref = f32[256,32]{1,0:T(8,128)} copy(f32[256,32]{0,1:T(8,128)S(1)} %copy-done.3) | data formatting | bytes 65536 | tf_op args[2]
  2.8 61.6 %shard_map.146 = (bf16[256,2048]{1,0:T(8,128)(2,1)}, bf16[256,2048]{1,0:T(8,128)(2,1)}, f32[256,32]{1,0:T(8,128)}, f32[256,256]{1,0:T(8,128)}, f32[256,256]{1,0:T(8,128)}) custom-call(bf16[256,2048]{1,0:T(8,128)(2,1)} %x_ref.1, bf16[256,2048]{1,0:T(8,128)(2,1)} %gate_ref.1, f32[256,32]{1,0:T(8,128)} %copy.16.step_ref, bf16[256,256]{1,0:T(8,128)(2,1)} %b_ref.1, ...), custom_call_target="tpu_custom_call" | custom-call | tf_op jit(solution)/shard_map/pallas_call | solution.py:432
  64.4 1.6 %copy.17 = f32[256,32]{0,1:T(8,128)} copy(f32[256,32]{1,0:T(8,128)} %get-tuple-element.7) | data formatting | bytes 65536 | tf_op jit(solution)/shard_map/pallas_call | solution.py:432
  66.0 0.0 copy-start
  66.0 2.4 %copy.22 = bf16[256,2048]{1,0:T(8,128)(2,1)} copy(bf16[256,2048]{1,0:T(8,128)(2,1)} %get-tuple-element.15) | data formatting | bytes 2097152
  68.4 0.0 copy-done
  68.4 0.0 copy-start.2
  68.4 1.0 %copy.23 = bf16[256,2048]{1,0:T(8,128)(2,1)} copy(bf16[256,2048]{1,0:T(8,128)(2,1)S(1)} %copy-done) | data formatting | bytes 2097152
  69.4 0.1 copy-done.2
  69.5 0.0 copy-start.1
  69.5 0.7 copy.24
  70.2 0.3 copy-done.1
  70.6 0.7 copy.25
Async XLA Ops:
  0.6 1.4 %copy-start.3 = (f32[256,32]{0,1:T(8,128)S(1)}, f32[256,32]{0,1:T(8,128)}, u32[]{:S(2)}) copy-start(f32[256,32]{0,1:T(8,128)} %param.13) | copy-start | bytes 98308
  66.0 2.4 %copy-start = (bf16[256,2048]{1,0:T(8,128)(2,1)S(1)}, bf16[256,2048]{1,0:T(8,128)(2,1)}, u32[]{:S(2)}) copy-start(bf16[256,2048]{1,0:T(8,128)(2,1)} %get-tuple-element.16) | copy-start | bytes 3145732
  68.4 1.1 %copy-start.2 = (f32[256,256]{1,0:T(8,128)S(1)}, f32[256,256]{1,0:T(8,128)}, u32[]{:S(2)}) copy-start(f32[256,256]{1,0:T(8,128)} %get-tuple-element.18) | copy-start | bytes 786436
  69.5 1.0 %copy-start.1 = (f32[256,256]{1,0:T(8,128)S(1)}, f32[256,256]{1,0:T(8,128)}, u32[]{:S(2)}) copy-start(f32[256,256]{1,0:T(8,128)} %get-tuple-element.19) | copy-start | bytes 786436
